TPU v7x, 768 devices: a whole 4x8x12 slice. The times are simulated.
768 devices in a mesh: dp: 24 (over y_lo, z), tensor: 32 (over x, y_hi, core).
Axes of the slice: x: 4, y: 8 (y_hi: 4, y_lo: 2; y = y_hi * 2 + y_lo), z: 12, core: 2. Of those that a mesh axis runs over, the one named last changes fastest.
Arguments:
- expert_rows: bfloat16 [24, 32, 1056, 768], P('dp', 'tensor'), may hold values from -0.109375 to 0.109375
- expert_ids: int32 [98304, 2], P(('dp', 'tensor')), may hold values from 0 to 7, all different within a row; in each aligned block of 128 rows (0 to 127, 128 to 255, ...) at most 33 rows name the same one
- gate_logits: float32 [98304, 2], P(('dp', 'tensor')), may hold values from -6 to 6
- layer_input: bfloat16 [98304, 3072], P(('dp', 'tensor')), may hold values from -24 to 24
- out_grad: bfloat16 [98304, 3072], P(('dp', 'tensor')), may hold values from -6 to 6
Outputs:
- slot_grad: bfloat16 [24, 32, 1056, 768], P('dp', 'tensor')
- logit_grad: float32 [98304, 2], P(('dp', 'tensor'))
- router_grad: float32 [3072, 8], P(('dp', 'tensor'))
Inputs may be any that keep to these rules, and one draw needn't show every extreme that they name: `expert_ids`: the two experts of a token differ. Among the 128 rows of one device no expert is named by more than 33 rows, and in some devices one expert is named by exactly 33 rows.
All inputs are finite; a program needn't handle non-finite values.
Results may differ from a plain program's by a relative error of at most 0.0029.
Values may be sent and summed in bfloat16 or wider, within the bound.
A program may use at most 64 MiB of HBM per device.

v0:
```python
import jax
import jax.numpy as jnp
from jax import lax
from jax.sharding import PartitionSpec as P

EXPERTS = 8


def on_device(expert_rows, expert_ids, gate_logits, layer_input, out_grad):
    tensor_size = lax.axis_size("tensor")
    group_count = lax.axis_size("dp")
    members = tensor_size // EXPERTS
    slot_count = expert_rows.shape[2]
    span_cols = expert_rows.shape[3]
    capacity = slot_count // tensor_size
    tok_rows, width = out_grad.shape
    catalog = jnp.arange(EXPERTS, dtype=jnp.int32)
    chosen = (expert_ids[:, :, None] == catalog[None, None, :]).astype(jnp.int32)
    hit_counts = jnp.sum(chosen, axis=1)
    before = jnp.cumsum(hit_counts, axis=0) - hit_counts
    slot_rank = jnp.take_along_axis(before, expert_ids, axis=1)
    target = (expert_ids * capacity + slot_rank).reshape(-1)
    placing = (target[None, :] == jnp.arange(EXPERTS * capacity, dtype=jnp.int32)[:, None]).astype(
        jnp.bfloat16
    )
    first_prob = 1.0 / (1.0 + jnp.exp(gate_logits[:, 1] - gate_logits[:, 0]))
    second_prob = 1.0 / (1.0 + jnp.exp(gate_logits[:, 0] - gate_logits[:, 1]))
    weights = jnp.stack([first_prob, second_prob], axis=1)
    grad32 = out_grad.astype(jnp.float32)
    own_slots = expert_rows[0, 0]
    scaled = (
        (weights[:, :, None] * grad32[:, None, :]).astype(jnp.bfloat16).reshape(tok_rows * 2, width)
    )
    packed = jnp.dot(placing, scaled, preferred_element_type=jnp.float32).astype(jnp.bfloat16)
    outgoing = (
        packed.reshape(EXPERTS, capacity, members, span_cols)
        .transpose(0, 2, 1, 3)
        .reshape(tensor_size, capacity, span_cols)
    )
    slot_blocks = own_slots.reshape(tensor_size, capacity, span_cols)
    arrived_rows = lax.all_to_all(slot_blocks, "tensor", split_axis=0, concat_axis=0, tiled=True)
    arrived_grads = lax.all_to_all(outgoing, "tensor", split_axis=0, concat_axis=0, tiled=True)
    by_expert = (
        arrived_rows.reshape(EXPERTS, members, capacity, span_cols)
        .transpose(0, 2, 1, 3)
        .reshape(EXPERTS * capacity, width)
    )
    fetched = jnp.take(by_expert, target, axis=0)
    fetched = fetched.reshape(tok_rows, 2, width)
    scores = jnp.sum(fetched.astype(jnp.float32) * grad32[:, None, :], axis=2)
    slot_grad = arrived_grads.reshape(1, 1, slot_count, span_cols)
    average = jnp.sum(weights * scores, axis=1, keepdims=True)
    logit_grad = weights * (scores - average)
    combined = jnp.sum(chosen.astype(jnp.float32) * logit_grad[:, :, None], axis=1).astype(
        jnp.bfloat16
    )
    total_tokens = tok_rows * group_count * tensor_size
    router_grad = lax.psum_scatter(
        lax.dot_general(
            layer_input, combined, (((0,), (0,)), ((), ())), preferred_element_type=jnp.float32
        ),
        ("dp", "tensor"),
        scatter_dimension=0,
        tiled=True,
    ) * total_tokens ** (-0.5)
    return (slot_grad, logit_grad, router_grad)


def solution(mesh):
    in_specs = (
        P("dp", "tensor", None, None),
        P(("dp", "tensor"), None),
        P(("dp", "tensor"), None),
        P(("dp", "tensor"), None),
        P(("dp", "tensor"), None),
    )
    out_specs = (
        P("dp", "tensor", None, None),
        P(("dp", "tensor"), None),
        P(("dp", "tensor"), None),
    )
    return jax.shard_map(
        on_device, mesh=mesh, in_specs=in_specs, out_specs=out_specs, check_vma=False
    )
```

profile of v0, /device:TPU:1, one launch (start us, length us, event | category | flops | bytes accessed | tf_op | source)
XLA Modules:
  0.0 558.6 jit_solution(399563207244976882)
XLA Ops:
  7.2 2.8 reshape_squeeze.3
  10.0 15.0 %all-to-all-start.1 = ((bf16[32,33,768]{2,1,0:T(8,128)(2,1)}), bf16[32,33,768]{2,1,0:T(8,128)(2,1)}, u32[]{:S(2)}, u32[]{:S(2)}) async-start(bf16[32,33,768]{2,1,0:T(8,128)(2,1)} %reshape_squeeze.3), calls=%async_computation.1 | async-start | bytes 3932160 | tf_op jit(solution)/shard_map/all_to_all | solution.py:41
  25.1 0.2 reduce_window_sum.11
  25.3 0.1 copy.67
  25.4 0.1 reshape.142
  25.6 1.9 gather_fusion.1
  27.5 0.1 reshape.145
  27.8 0.1 copy.69
  27.9 2.5 mul.61
  30.4 5.2 mul.62
  35.7 0.1 copy.70
  35.8 0.1 eq.31
  36.0 0.1 mul.59
  36.1 2.6 convolution_convert_fusion
  38.7 2.4 reshape.128
  41.1 3.0 copy.82
  44.1 27.4 %all-to-all-done.1 = bf16[32,33,768]{2,1,0:T(8,128)(2,1)} async-done(((bf16[32,33,768]{2,1,0:T(8,128)(2,1)}), bf16[32,33,768]{2,1,0:T(8,128)(2,1)}, u32[]{:S(2)}, u32[]{:S(2)}) %all-to-all-start.1) | async-done | bytes 1622048 | tf_op jit(solution)/shard_map/all_to_all | solution.py:41
  71.4 5.6 %all-to-all-start = ((bf16[32,33,768]{2,1,0:T(8,128)(2,1)}), bf16[32,33,768]{2,1,0:T(8,128)(2,1)}, u32[]{:S(2)}, u32[]{:S(2)}) async-start(bf16[32,33,768]{2,1,0:T(8,128)(2,1)} %bitcast.2), calls=%async_computation | async-start | bytes 3932160 | tf_op jit(solution)/shard_map/all_to_all | solution.py:42
  77.1 0.1 reshape.133
  77.3 0.1 copy.73
  77.4 0.2 broadcast_in_dim.25
  77.6 2.2 copy.84
  79.8 0.3 copy.88
  80.0 2.7 gather_fusion
  82.7 2.9 multiply_reduce_fusion
  85.7 0.1 reduce_sum.40
  86.1 0.9 convolution_bitcast_fusion
  87.0 38.1 %all-to-all-done = bf16[32,33,768]{2,1,0:T(8,128)(2,1)} async-done(((bf16[32,33,768]{2,1,0:T(8,128)(2,1)}), bf16[32,33,768]{2,1,0:T(8,128)(2,1)}, u32[]{:S(2)}, u32[]{:S(2)}) %all-to-all-start) | async-done | bytes 1622048 | tf_op jit(solution)/shard_map/all_to_all | solution.py:42
  125.1 2.7 reshape.130
  127.8 422.6 %all-reduce.3.cloned.1.call-done = f32[3072,8]{0,1:T(8,128)} async-done(((f32[3072,8]{0,1:T(8,128)}), f32[3072,8]{0,1:T(8,128)}) %all-reduce.3.cloned.1.call-update) | async-done | bytes 98320
  550.4 0.8 dynamic-slice_multiply_fusion
  551.1 0.7 copy.81
  (26 shorter events, 0.6 us)
Async XLA Ops:
  7.2 78.9 %copy-start = (bf16[128,3072]{1,0:T(8,128)(2,1)S(1)}, bf16[128,3072]{1,0:T(8,128)(2,1)}, u32[]{:S(2)}) copy-start(bf16[128,3072]{1,0:T(8,128)(2,1)} %param.8) | copy-start | bytes 2359300
  10.0 15.0 %copy-start.2 = (s32[128,2]{0,1:T(2,128)S(1)}, s32[128,2]{0,1:T(2,128)}, u32[]{:S(2)}) copy-start(s32[128,2]{0,1:T(2,128)} %param.6) | copy-start | bytes 3076
  10.0 61.4 %all-to-all-start.1 = ((bf16[32,33,768]{2,1,0:T(8,128)(2,1)}), bf16[32,33,768]{2,1,0:T(8,128)(2,1)}, u32[]{:S(2)}, u32[]{:S(2)}) async-start(bf16[32,33,768]{2,1,0:T(8,128)(2,1)} %reshape_squeeze.3), calls=%async_computation.1 | async-start | bytes 3932160 | tf_op jit(solution)/shard_map/all_to_all | solution.py:41
  25.6 2.3 copy-start.1
  30.4 5.3 copy-start.4
  71.4 53.7 %all-to-all-start = ((bf16[32,33,768]{2,1,0:T(8,128)(2,1)}), bf16[32,33,768]{2,1,0:T(8,128)(2,1)}, u32[]{:S(2)}, u32[]{:S(2)}) async-start(bf16[32,33,768]{2,1,0:T(8,128)(2,1)} %bitcast.2), calls=%async_computation | async-start | bytes 3932160 | tf_op jit(solution)/shard_map/all_to_all | solution.py:42
  77.1 473.3 %all-reduce.3.cloned.1.call-start = ((), (), s32[]{:S(2)}) async-start(), calls=%async_computation.2 | async-start | bytes 196608
  86.1 41.7 %copy-start.3 = (f32[128,2]{0,1:T(2,128)}, f32[128,2]{0,1:T(2,128)S(1)}, u32[]{:S(2)}) copy-start(f32[128,2]{0,1:T(2,128)S(1)} %copy.80) | copy-start | bytes 3076
Sparse Core Ops, SparseCore 0:
  87.1 463.1 all-reduce.2
where the time goes:
time: 560 us; the launch traced here: 559 us
  waiting for transfers between devices  488 us (87%)
  local copies, waits for them, and re-layouts  28.1 us (5%)
  starting transfers between devices  20.6 us (4%)
  between operations  14.2 us (3%)
    unnamed x2, waiting for transfers between devices  423 us
    all_to_all x1, waiting for transfers between devices, on_device(): lax.all_to_all(outgoing, 'tensor', split_axis=0, concat_axis=0, tiled=True)  38.1 us
    all_to_all x1, waiting for transfers between devices, on_device(): lax.all_to_all(slot_blocks, 'tensor', split_axis=0, concat_axis=0, tiled=...  27.4 us
    all_to_all x1, starting transfers between devices, on_device(): lax.all_to_all(slot_blocks, 'tensor', split_axis=0, concat_axis=0, tiled=...  15 us
  transfers between devices with their start and end apart: 3, of which 3 were waited for; matrix products, arithmetic and copies ran while one was open for 6% of the time, Pallas kernels for 0%

commit v1 on v0

v1 whole, which is shorter than its diff:
```python
import functools

import jax
import jax.numpy as jnp
from jax import lax
from jax.experimental import pallas as pl
from jax.experimental.pallas import tpu as pltpu
from jax.sharding import PartitionSpec as P

EXPERTS = 8
LANES = 128
F32 = jnp.float32
BF16 = jnp.bfloat16
MESH = pl.DeviceIdType.MESH


def iota(shape, axis):
    return lax.broadcasted_iota(jnp.int32, shape, axis)


def split3(x):
    hi = x.astype(BF16).astype(F32)
    mid = (x - hi).astype(BF16).astype(F32)
    return hi, mid, x - hi - mid


def kernel(
    n_dp,
    n_tensor,
    scale,
    rows_hbm,
    ids_ref,
    logits_ref,
    input_hbm,
    grad_hbm,
    slot_out,
    logit_out,
    router_out,
    rows,
    inputs,
    grads,
    send,
    recv,
    rows32,
    slot32,
    score_send,
    score_recv,
    term_send,
    term_recv,
    turned,
    part_send,
    part_recv,
    load_sem,
    send_sem,
    recv_sem,
    ssend_sem,
    srecv_sem,
    tsend_sem,
    trecv_sem,
    psend_sem,
    precv_sem,
):
    me = lax.axis_index("tensor")
    group = lax.axis_index("dp")
    members = n_tensor // EXPERTS
    capacity = rows.shape[0] // n_tensor
    full = capacity - 1
    segments = rows.shape[1] // LANES
    body = full * segments
    tokens = grads.shape[0]

    load_grads = pltpu.make_async_copy(grad_hbm, grads, load_sem.at[0])
    load_rows = pltpu.make_async_copy(rows_hbm, rows, load_sem.at[1])
    load_inputs = pltpu.make_async_copy(input_hbm, inputs, load_sem.at[2])
    load_grads.start()
    load_rows.start()
    load_inputs.start()

    barrier = pltpu.get_barrier_semaphore()

    @pl.loop(1, n_tensor)
    def _(i):
        peer = lax.rem(me + i, n_tensor)
        pl.semaphore_signal(barrier, inc=1, device_id={"tensor": peer}, device_id_type=MESH)

    @pl.loop(1, n_dp)
    def _(i):
        peer = lax.rem(group + i, n_dp)
        pl.semaphore_signal(barrier, inc=1, device_id={"dp": peer}, device_id_type=MESH)

    id0, id1 = ids_ref[0:1, :], ids_ref[1:2, :]
    logit0, logit1 = logits_ref[0:1, :], logits_ref[1:2, :]
    prob0 = 1.0 / (1.0 + jnp.exp(logit1 - logit0))
    prob1 = 1.0 / (1.0 + jnp.exp(logit0 - logit1))
    experts = iota((EXPERTS, tokens), 0)
    hot0 = jnp.where(experts == id0, 1.0, 0.0)
    hot1 = jnp.where(experts == id1, 1.0, 0.0)
    earlier = jnp.where(
        iota((tokens, tokens), 0) < iota((tokens, tokens), 1), 1.0, 0.0
    ).astype(BF16)
    before = jnp.dot((hot0 + hot1).astype(BF16), earlier, preferred_element_type=F32)
    rank0 = jnp.sum(hot0 * before, axis=0, keepdims=True).astype(jnp.int32)
    rank1 = jnp.sum(hot1 * before, axis=0, keepdims=True).astype(jnp.int32)
    slots = iota((LANES, tokens), 0)
    tail_row = iota((16, LANES), 0)

    load_grads.wait()
    pl.semaphore_wait(barrier, n_tensor - 1 + n_dp - 1)

    def remote_block(index, peer):
        return pltpu.make_async_remote_copy(
            src_ref=send.at[peer],
            dst_ref=recv.at[index],
            send_sem=send_sem.at[peer],
            recv_sem=recv_sem.at[index],
            device_id={"tensor": peer},
            device_id_type=MESH,
        )

    def pair(i):
        step = lax.rem(i // 2 + 1, 4)
        return step, lax.rem(i, 2)

    my_expert = me // members

    def expert_at(i, sign):
        step, other = pair(i)
        column = lax.rem(my_expert // 2 + sign * step + 4, 4)
        half = lax.rem(lax.rem(my_expert, 2) + other, 2)
        return column * 2 + half

    @pl.loop(0, EXPERTS)
    def _(i):
        expert = expert_at(i, 1)
        key0 = jnp.where(id0 == expert, rank0, -1)
        key1 = jnp.where(id1 == expert, rank1, -1)
        placing = jnp.where((slots == key0) | (slots == key1), 1.0, 0.0).astype(BF16)
        prob = jnp.where(id0 == expert, prob0, jnp.where(id1 == expert, prob1, 0.0))
        hi, mid, lo = split3(prob)
        parts = jnp.where(
            tail_row == segments,
            hi,
            jnp.where(tail_row == segments + 1, mid, jnp.where(tail_row == segments + 2, lo, 0.0)),
        ).astype(BF16)
        slot_probs = lax.dot_general(
            parts, placing, (((1,), (1,)), ((), ())), preferred_element_type=F32
        )
        for k in range(members):
            peer = expert * members + k
            packed = jnp.dot(
                placing[: full + 16],
                grads[:, k * segments * LANES : (k + 1) * segments * LANES],
                preferred_element_type=F32,
            )
            tail = slot_probs
            for j in range(segments):
                piece = packed[:, j * LANES : (j + 1) * LANES]
                send[peer, j * full : (j + 1) * full, :] = piece[:full].astype(BF16)
                tail = jnp.where(tail_row == j, piece[full : full + 1], tail)
            send[peer, body : body + 16, :] = tail.astype(BF16)

            @pl.when(peer != me)
            def _():
                remote_block(me, peer).start()

            @pl.when(peer == me)
            def _():
                pltpu.make_async_copy(send.at[me], recv.at[me], recv_sem.at[me]).start()

    load_rows.wait()

    @pl.loop(0, rows.shape[0] // 32)
    def _(i):
        at = pl.multiple_of(i * 32, 32)
        for j in range(segments):
            rows32[j, pl.ds(at, 32), :] = rows[
                pl.ds(at, 32), j * LANES : (j + 1) * LANES
            ].astype(F32)

    diagonal = iota((full, LANES), 0) == iota((full, LANES), 1)
    lane = iota((1, LANES), 1)

    def remote_scores(index, peer):
        return pltpu.make_async_remote_copy(
            src_ref=score_send.at[peer],
            dst_ref=score_recv.at[index],
            send_sem=ssend_sem.at[peer],
            recv_sem=srecv_sem.at[index],
            device_id={"tensor": peer},
            device_id_type=MESH,
        )

    @pl.loop(0, n_tensor)
    def _(i):
        source = expert_at(i // members, -1) * members + lax.rem(i, members)
        pltpu.make_async_copy(send.at[source], recv.at[source], recv_sem.at[source]).wait()
        at = source * capacity
        tail = recv[source, body : body + 16, :].astype(F32)
        prob = (
            tail[segments : segments + 1]
            + tail[segments + 1 : segments + 2]
            + tail[segments + 2 : segments + 3]
        )
        prob_column = jnp.sum(jnp.where(diagonal, prob, 0.0), axis=1, keepdims=True)
        prob_last = jnp.sum(jnp.where(lane == full, prob, 0.0), axis=1, keepdims=True)
        products = jnp.zeros((full, LANES), F32)
        last = jnp.zeros((1, LANES), F32)
        for j in range(segments):
            piece = recv[source, j * full : (j + 1) * full, :].astype(F32)
            products += piece * rows32[j, pl.ds(at, full), :]
            slot32[j, pl.ds(at, full), :] = piece * prob_column
            row = tail[j : j + 1]
            last += row * rows32[j, pl.ds(at + full, 1), :]
            slot32[j, pl.ds(at + full, 1), :] = row * prob_last
        sums = jnp.sum(products, axis=1, keepdims=True)
        line = jnp.sum(jnp.where(diagonal, sums, 0.0), axis=0, keepdims=True)
        last_sum = jnp.sum(last, axis=1, keepdims=True)
        score_send[source] = jnp.where(lane == full, last_sum, line)

        @pl.when(source != me)
        def _():
            remote_scores(me, source).start()

        @pl.when(source == me)
        def _():
            pltpu.make_async_copy(
                score_send.at[me], score_recv.at[me], srecv_sem.at[me]
            ).start()

    ranks = iota((LANES, tokens), 0)
    chosen0 = jnp.where(ranks == rank0, 1.0, 0.0).astype(BF16)
    chosen1 = jnp.where(ranks == rank1, 1.0, 0.0).astype(BF16)
    load_inputs.wait()

    @pl.loop(0, n_tensor)
    def _(i):
        pltpu.make_async_copy(score_send.at[i], score_recv.at[i], srecv_sem.at[i]).wait()

    scores = jnp.zeros((EXPERTS, LANES), F32)
    for expert in range(EXPERTS):
        total = score_recv[expert * members]
        for k in range(1, members):
            total += score_recv[expert * members + k]
        scores = jnp.where(iota((EXPERTS, LANES), 0) == expert, total, scores)
    hi, mid, lo = split3(scores)
    terms = [part.astype(BF16) for part in (hi, mid, lo)]

    def looked_up(chosen, hot):
        found = jnp.zeros((EXPERTS, tokens), F32)
        for term in terms:
            found += jnp.dot(term, chosen, preferred_element_type=F32)
        return jnp.sum(found * hot, axis=0, keepdims=True)

    score0 = looked_up(chosen0, hot0)
    score1 = looked_up(chosen1, hot1)
    average = prob0 * score0 + prob1 * score1
    slope0 = prob0 * (score0 - average)
    slope1 = prob1 * (score1 - average)
    logit_out[0:1, :] = slope0
    logit_out[1:2, :] = slope1
    combined = (hot0 * slope0 + hot1 * slope1).astype(BF16)

    for g in range(n_dp):
        term_send[g] = jnp.dot(
            combined, inputs[:, g * LANES : (g + 1) * LANES], preferred_element_type=F32
        )

    def remote_term(index, peer):
        return pltpu.make_async_remote_copy(
            src_ref=term_send.at[peer],
            dst_ref=term_recv.at[index],
            send_sem=tsend_sem.at[peer],
            recv_sem=trecv_sem.at[index],
            device_id={"dp": peer},
            device_id_type=MESH,
        )

    @pl.loop(1, n_dp)
    def _(i):
        remote_term(group, lax.rem(group + i, n_dp)).start()

    own_term = pltpu.make_async_copy(
        term_send.at[group], term_recv.at[group], trecv_sem.at[group]
    )
    own_term.start()

    @pl.loop(0, rows.shape[0] // 32)
    def _(i):
        at = pl.multiple_of(i * 32, 32)
        for j in range(segments):
            slot_out[pl.ds(at, 32), j * LANES : (j + 1) * LANES] = slot32[
                j, pl.ds(at, 32), :
            ].astype(BF16)

    @pl.loop(0, n_dp)
    def _(i):
        pltpu.make_async_copy(term_send.at[i], term_recv.at[i], trecv_sem.at[i]).wait()

    total = term_recv[0]
    for g in range(1, n_dp):
        total += term_recv[g]

    square = jnp.concatenate([total, jnp.zeros((LANES - EXPERTS, LANES), F32)], axis=0)
    turned[...] = jnp.transpose(square)
    owned = LANES // n_tensor
    lines = turned[pl.ds(0, n_tensor, stride=owned), :]
    for j in range(1, owned):
        lines += pltpu.roll(turned[pl.ds(j, n_tensor, stride=owned), :], j * EXPERTS, 1)
    for i in range(n_tensor):
        part_send[i] = lines[i : i + 1]

    def remote_part(index, peer):
        return pltpu.make_async_remote_copy(
            src_ref=part_send.at[peer],
            dst_ref=part_recv.at[index],
            send_sem=psend_sem.at[peer],
            recv_sem=precv_sem.at[index],
            device_id={"tensor": peer},
            device_id_type=MESH,
        )

    @pl.loop(1, n_tensor)
    def _(i):
        remote_part(me, lax.rem(me + i, n_tensor)).start()

    own_part = pltpu.make_async_copy(part_send.at[me], part_recv.at[me], precv_sem.at[me])
    own_part.start()

    @pl.loop(1, n_tensor)
    def _(i):
        peer = lax.rem(me + i, n_tensor)
        remote_block(me, peer).wait_send()
        remote_scores(me, peer).wait_send()

    @pl.loop(1, n_dp)
    def _(i):
        remote_term(group, lax.rem(group + i, n_dp)).wait_send()

    @pl.loop(0, n_tensor)
    def _(i):
        pltpu.make_async_copy(part_send.at[i], part_recv.at[i], precv_sem.at[i]).wait()

    line = part_recv[0]
    for i in range(1, n_tensor):
        line += part_recv[i]
    line = line * scale
    for j in range(owned):
        router_out[j : j + 1, :] = line[:, j * EXPERTS : (j + 1) * EXPERTS]

    @pl.loop(1, n_tensor)
    def _(i):
        remote_part(me, lax.rem(me + i, n_tensor)).wait_send()


def on_device(expert_rows, expert_ids, gate_logits, layer_input, out_grad):
    n_tensor = lax.axis_size("tensor")
    n_dp = lax.axis_size("dp")
    slot_count, span = expert_rows.shape[2:]
    tokens, width = out_grad.shape
    capacity = slot_count // n_tensor
    segments = span // LANES
    block = (capacity - 1) * segments + 16
    owned = width // (n_dp * n_tensor)
    padded = slot_count + 8
    any_space = pl.BlockSpec(memory_space=pl.ANY)
    in_vmem = pl.BlockSpec(memory_space=pltpu.VMEM)
    dma = pltpu.SemaphoreType.DMA
    slot_grad, logit_grad, router_grad = pl.pallas_call(
        functools.partial(kernel, n_dp, n_tensor, (tokens * n_dp * n_tensor) ** -0.5),
        out_shape=(
            jax.ShapeDtypeStruct((slot_count, span), BF16),
            jax.ShapeDtypeStruct((2, tokens), F32),
            jax.ShapeDtypeStruct((owned, EXPERTS), F32),
        ),
        in_specs=[any_space, in_vmem, in_vmem, any_space, any_space],
        out_specs=(in_vmem, in_vmem, in_vmem),
        scratch_shapes=[
            pltpu.VMEM((slot_count, span), BF16),
            pltpu.VMEM((tokens, width), BF16),
            pltpu.VMEM((tokens, width), BF16),
            pltpu.VMEM((n_tensor, block, LANES), BF16),
            pltpu.VMEM((n_tensor, block, LANES), BF16),
            pltpu.VMEM((segments, padded, LANES), F32),
            pltpu.VMEM((segments, padded, LANES), F32),
            pltpu.VMEM((n_tensor, 1, LANES), F32),
            pltpu.VMEM((n_tensor, 1, LANES), F32),
            pltpu.VMEM((n_dp, EXPERTS, LANES), F32),
            pltpu.VMEM((n_dp, EXPERTS, LANES), F32),
            pltpu.VMEM((LANES, LANES), F32),
            pltpu.VMEM((n_tensor, 1, LANES), F32),
            pltpu.VMEM((n_tensor, 1, LANES), F32),
            dma((3,)),
            dma((n_tensor,)),
            dma((n_tensor,)),
            dma((n_tensor,)),
            dma((n_tensor,)),
            dma((n_dp,)),
            dma((n_dp,)),
            dma((n_tensor,)),
            dma((n_tensor,)),
        ],
        compiler_params=pltpu.CompilerParams(
            collective_id=0, has_side_effects=True, vmem_limit_bytes=56 * 2**20
        ),
    )(
        expert_rows.reshape(slot_count, span),
        expert_ids.T,
        gate_logits.T,
        layer_input,
        out_grad,
    )
    return slot_grad.reshape(expert_rows.shape), logit_grad.T, router_grad


def solution(mesh):
    in_specs = (
        P("dp", "tensor", None, None),
        P(("dp", "tensor"), None),
        P(("dp", "tensor"), None),
        P(("dp", "tensor"), None),
        P(("dp", "tensor"), None),
    )
    out_specs = (
        P("dp", "tensor", None, None),
        P(("dp", "tensor"), None),
        P(("dp", "tensor"), None),
    )
    return jax.shard_map(
        on_device, mesh=mesh, in_specs=in_specs, out_specs=out_specs, check_vma=False
    )
```

time: 560 us -> 87.8 us (0.16)
  waiting for transfers between devices: 488 us -> 0 us
  Pallas kernels: 0 us -> 83.1 us
  local copies, waits for them, and re-layouts: 28.1 us -> 3.84 us
  starting transfers between devices: 20.6 us -> 0 us
  between operations: 14.2 us -> 0.66 us
    unnamed x2 -> x0, waiting for transfers between devices: 423 us -> none
    pallas_call x0 -> x1, Pallas kernels: none -> 83.1 us  [on_device(): pl.pallas_call(functools.partial(kernel, n_dp, n_tensor, (tokens * n_dp *...]
    all_to_all x2 -> x0, waiting for transfers between devices: 65.5 us -> none  [the longest x1 38.1 us: on_device(): lax.all_to_all(outgoing, 'tensor', split_axis=0, concat_axis=0, tiled=True)]
    all_to_all x2 -> x0, starting transfers between devices: 20.6 us -> none  [the longest x1 15 us: on_device(): lax.all_to_all(slot_blocks, 'tensor', split_axis=0, concat_axis=0, tiled=...]
    reshape x4 -> x0, local copies, waits for them, and re-layouts: 8.22 us -> none  [the longest x1 3 us: on_device(): outgoing = packed.reshape(EXPERTS, capacity, members, span_cols).transpos...]
    mul x3 -> x0, local copies, waits for them, and re-layouts: 7.91 us -> none  [on_device(): weights[:, :, None] * grad32[:, None, :]]
  transfers between devices with their start and end apart: 3 -> 0, of which waited for: 3 -> 0; matrix products, arithmetic and copies ran while one was open for 6% -> 0% of each run, Pallas kernels for 0% -> 0%
where the time goes in v1:
time: 87.8 us; the launch traced here: 87.6 us
  Pallas kernels  83.1 us (95%)
  local copies, waits for them, and re-layouts  3.84 us (4%)
    pallas_call x1, Pallas kernels, on_device(): pl.pallas_call(functools.partial(kernel, n_dp, n_tensor, (tokens * n_dp *...  83.1 us
    unnamed x7, local copies, waits for them, and re-layouts  3.84 us

profile of v1, /device:TPU:1, one launch (start us, length us, event | category | flops | bytes accessed | tf_op | source)
XLA Modules:
  0.0 87.6 jit_solution(1529774109708583353)
XLA Ops:
  0.6 83.1 %shard_map.76 = (bf16[1056,768]{1,0:T(8,128)(2,1)}, f32[2,128]{1,0:T(2,128)}, f32[4,8]{1,0:T(4,128)}) custom-call(bf16[1056,768]{1,0:T(8,128)(2,1)} %bitcast.5, s32[2,128]{1,0:T(2,128)} %bitcast.7, f32[2,128]{1,0:T(2,128)} %bitcast.8, bf16[128,3072]{1,0:T(8,128)(2,1)} %input_hbm.1, bf16[128,3072]{1,0:T(8,128)(2,1)} %grad_hbm.1), custom_call_target="tpu_custom_call" | custom-call | tf_op jit(solution)/shard_map/pallas_call | solution.py:368
  83.7 0.0 copy-start.1
  83.7 0.0 copy-start
  83.8 2.7 %copy.11 = bf16[1,1,1056,768]{3,2,1,0:T(8,128)(2,1)} copy(bf16[1,1,1056,768]{3,2,1,0:T(8,128)(2,1)} %bitcast.6) | data formatting | bytes 3244032
  86.4 0.0 copy-done.1
  86.4 0.6 copy.12
  87.0 0.0 copy-done
  87.0 0.6 copy.13
Async XLA Ops:
  83.7 2.7 %copy-start.1 = (f32[2,128]{1,0:T(2,128)S(1)}, f32[2,128]{1,0:T(2,128)}, u32[]{:S(2)}) copy-start(f32[2,128]{1,0:T(2,128)} %get-tuple-element.7) | copy-start | bytes 3076
  83.7 3.3 %copy-start = (f32[4,8]{1,0:T(4,128)S(1)}, f32[4,8]{1,0:T(4,128)}, u32[]{:S(2)}) copy-start(f32[4,8]{1,0:T(4,128)} %get-tuple-element.14) | copy-start | bytes 388

commit v2 on v1

--- a/solution.py
+++ b/solution.py
@@ -22,6 +22,10 @@
     hi = x.astype(BF16).astype(F32)
     mid = (x - hi).astype(BF16).astype(F32)
     return hi, mid, x - hi - mid
+
+
+def wrapped(index, size):
+    return jnp.where(index >= size, index - size, index)
 
 
 def kernel(
@@ -69,24 +73,30 @@
     body = full * segments
     tokens = grads.shape[0]
 
+    barrier = pltpu.get_barrier_semaphore()
+
+    def tensor_peer(i):
+        return wrapped(me + i, n_tensor)
+
+    def dp_peer(i):
+        return wrapped(group + i, n_dp)
+
+    @pl.loop(1, n_tensor, unroll=True)
+    def _(i):
+        pl.semaphore_signal(
+            barrier, inc=1, device_id={"tensor": tensor_peer(i)}, device_id_type=MESH
+        )
+
+    @pl.loop(1, n_dp, unroll=True)
+    def _(i):
+        pl.semaphore_signal(barrier, inc=1, device_id={"dp": dp_peer(i)}, device_id_type=MESH)
+
     load_grads = pltpu.make_async_copy(grad_hbm, grads, load_sem.at[0])
     load_rows = pltpu.make_async_copy(rows_hbm, rows, load_sem.at[1])
     load_inputs = pltpu.make_async_copy(input_hbm, inputs, load_sem.at[2])
     load_grads.start()
     load_rows.start()
     load_inputs.start()
-
-    barrier = pltpu.get_barrier_semaphore()
-
-    @pl.loop(1, n_tensor)
-    def _(i):
-        peer = lax.rem(me + i, n_tensor)
-        pl.semaphore_signal(barrier, inc=1, device_id={"tensor": peer}, device_id_type=MESH)
-
-    @pl.loop(1, n_dp)
-    def _(i):
-        peer = lax.rem(group + i, n_dp)
-        pl.semaphore_signal(barrier, inc=1, device_id={"dp": peer}, device_id_type=MESH)
 
     id0, id1 = ids_ref[0:1, :], ids_ref[1:2, :]
     logit0, logit1 = logits_ref[0:1, :], logits_ref[1:2, :]
@@ -117,21 +127,21 @@
             device_id_type=MESH,
         )
 
-    def pair(i):
-        step = lax.rem(i // 2 + 1, 4)
-        return step, lax.rem(i, 2)
-
-    my_expert = me // members
-
-    def expert_at(i, sign):
-        step, other = pair(i)
-        column = lax.rem(my_expert // 2 + sign * step + 4, 4)
-        half = lax.rem(lax.rem(my_expert, 2) + other, 2)
-        return column * 2 + half
-
-    @pl.loop(0, EXPERTS)
-    def _(i):
-        expert = expert_at(i, 1)
+    column, row, core = me // 8, lax.rem(me // 2, 4), lax.rem(me, 2)
+
+    def partner(i, sign):
+        part, place = i // 8, i - 8
+        middle = (part == 1) | (part == 2)
+        along_y = jnp.where(middle, 1 + 2 * lax.rem(i, 2), jnp.where(part == 0, 2, 0))
+        rest = jnp.where(middle, place // 2, lax.rem(i, 8))
+        along_x = lax.rem(rest // 2 + 1, 4)
+        return (
+            lax.rem(column + sign * along_x + 4, 4) * 8
+            + lax.rem(row + sign * along_y + 4, 4) * 2
+            + lax.rem(core + rest + 1, 2)
+        )
+
+    def pack(expert):
         key0 = jnp.where(id0 == expert, rank0, -1)
         key1 = jnp.where(id1 == expert, rank1, -1)
         placing = jnp.where((slots == key0) | (slots == key1), 1.0, 0.0).astype(BF16)
@@ -159,13 +169,23 @@
                 tail = jnp.where(tail_row == j, piece[full : full + 1], tail)
             send[peer, body : body + 16, :] = tail.astype(BF16)
 
-            @pl.when(peer != me)
-            def _():
-                remote_block(me, peer).start()
-
-            @pl.when(peer == me)
-            def _():
-                pltpu.make_async_copy(send.at[me], recv.at[me], recv_sem.at[me]).start()
+    half = row // 2
+
+    @pl.loop(0, 4)
+    def _(i):
+        pack(lax.rem(column + i + 1, 4) * 2 + 1 - half)
+        remote_block(me, partner(2 * i, 1)).start()
+        remote_block(me, partner(2 * i + 1, 1)).start()
+
+    @pl.loop(0, 4)
+    def _(i):
+        pack(lax.rem(column + i + 1, 4) * 2 + half)
+
+    @pl.loop(8, n_tensor - 1)
+    def _(i):
+        remote_block(me, partner(i, 1)).start()
+
+    pltpu.make_async_copy(send.at[me], recv.at[me], recv_sem.at[me]).start()
 
     load_rows.wait()
 
@@ -184,15 +204,15 @@
         return pltpu.make_async_remote_copy(
             src_ref=score_send.at[peer],
             dst_ref=score_recv.at[index],
-            send_sem=ssend_sem.at[peer],
-            recv_sem=srecv_sem.at[index],
+            send_sem=ssend_sem,
+            recv_sem=srecv_sem,
             device_id={"tensor": peer},
             device_id_type=MESH,
         )
 
     @pl.loop(0, n_tensor)
     def _(i):
-        source = expert_at(i // members, -1) * members + lax.rem(i, members)
+        source = partner(i, -1)
         pltpu.make_async_copy(send.at[source], recv.at[source], recv_sem.at[source]).wait()
         at = source * capacity
         tail = recv[source, body : body + 16, :].astype(F32)
@@ -224,7 +244,7 @@
         @pl.when(source == me)
         def _():
             pltpu.make_async_copy(
-                score_send.at[me], score_recv.at[me], srecv_sem.at[me]
+                score_send.at[me], score_recv.at[me], srecv_sem
             ).start()
 
     ranks = iota((LANES, tokens), 0)
@@ -232,10 +252,7 @@
     chosen1 = jnp.where(ranks == rank1, 1.0, 0.0).astype(BF16)
     load_inputs.wait()
 
-    @pl.loop(0, n_tensor)
-    def _(i):
-        pltpu.make_async_copy(score_send.at[i], score_recv.at[i], srecv_sem.at[i]).wait()
-
+    pltpu.make_async_copy(score_send, score_recv, srecv_sem).wait()
     scores = jnp.zeros((EXPERTS, LANES), F32)
     for expert in range(EXPERTS):
         total = score_recv[expert * members]
@@ -260,27 +277,31 @@
     logit_out[1:2, :] = slope1
     combined = (hot0 * slope0 + hot1 * slope1).astype(BF16)
 
-    for g in range(n_dp):
-        term_send[g] = jnp.dot(
-            combined, inputs[:, g * LANES : (g + 1) * LANES], preferred_element_type=F32
-        )
-
     def remote_term(index, peer):
         return pltpu.make_async_remote_copy(
             src_ref=term_send.at[peer],
             dst_ref=term_recv.at[index],
-            send_sem=tsend_sem.at[peer],
-            recv_sem=trecv_sem.at[index],
+            send_sem=tsend_sem,
+            recv_sem=trecv_sem,
             device_id={"dp": peer},
             device_id_type=MESH,
         )
 
-    @pl.loop(1, n_dp)
-    def _(i):
-        remote_term(group, lax.rem(group + i, n_dp)).start()
+    for k in range(members):
+        term = jnp.dot(
+            combined,
+            inputs[:, k * segments * LANES : (k + 1) * segments * LANES],
+            preferred_element_type=F32,
+        )
+        for j in range(segments):
+            term_send[k * segments + j] = term[:, j * LANES : (j + 1) * LANES]
+
+    @pl.loop(1, n_dp, unroll=True)
+    def _(i):
+        remote_term(group, dp_peer(i)).start()
 
     own_term = pltpu.make_async_copy(
-        term_send.at[group], term_recv.at[group], trecv_sem.at[group]
+        term_send.at[group], term_recv.at[group], trecv_sem
     )
     own_term.start()
 
@@ -292,10 +313,7 @@
                 j, pl.ds(at, 32), :
             ].astype(BF16)
 
-    @pl.loop(0, n_dp)
-    def _(i):
-        pltpu.make_async_copy(term_send.at[i], term_recv.at[i], trecv_sem.at[i]).wait()
-
+    pltpu.make_async_copy(term_send, term_recv, trecv_sem).wait()
     total = term_recv[0]
     for g in range(1, n_dp):
         total += term_recv[g]
@@ -313,33 +331,29 @@
         return pltpu.make_async_remote_copy(
             src_ref=part_send.at[peer],
             dst_ref=part_recv.at[index],
-            send_sem=psend_sem.at[peer],
-            recv_sem=precv_sem.at[index],
+            send_sem=psend_sem,
+            recv_sem=precv_sem,
             device_id={"tensor": peer},
             device_id_type=MESH,
         )
 
+    @pl.loop(1, n_tensor, unroll=True)
+    def _(i):
+        remote_part(me, tensor_peer(i)).start()
+
+    own_part = pltpu.make_async_copy(part_send.at[me], part_recv.at[me], precv_sem)
+    own_part.start()
+
     @pl.loop(1, n_tensor)
     def _(i):
-        remote_part(me, lax.rem(me + i, n_tensor)).start()
-
-    own_part = pltpu.make_async_copy(part_send.at[me], part_recv.at[me], precv_sem.at[me])
-    own_part.start()
-
-    @pl.loop(1, n_tensor)
-    def _(i):
-        peer = lax.rem(me + i, n_tensor)
-        remote_block(me, peer).wait_send()
-        remote_scores(me, peer).wait_send()
-
-    @pl.loop(1, n_dp)
-    def _(i):
-        remote_term(group, lax.rem(group + i, n_dp)).wait_send()
-
-    @pl.loop(0, n_tensor)
-    def _(i):
-        pltpu.make_async_copy(part_send.at[i], part_recv.at[i], precv_sem.at[i]).wait()
-
+        remote_block(me, tensor_peer(i)).wait_send()
+
+    others = pl.ds(0, n_tensor - 1)
+    pltpu.make_async_copy(score_send.at[others], score_recv.at[others], ssend_sem).wait()
+    others_dp = pl.ds(0, n_dp - 1)
+    pltpu.make_async_copy(term_send.at[others_dp], term_recv.at[others_dp], tsend_sem).wait()
+
+    pltpu.make_async_copy(part_send, part_recv, precv_sem).wait()
     line = part_recv[0]
     for i in range(1, n_tensor):
         line += part_recv[i]
@@ -347,9 +361,22 @@
     for j in range(owned):
         router_out[j : j + 1, :] = line[:, j * EXPERTS : (j + 1) * EXPERTS]
 
-    @pl.loop(1, n_tensor)
-    def _(i):
-        remote_part(me, lax.rem(me + i, n_tensor)).wait_send()
+    pltpu.make_async_copy(part_send.at[others], part_recv.at[others], psend_sem).wait()
+
+
+def hand_over(chunks, slots, logits, router, slots_out, logits_out, router_out, sem):
+    rows = slots.shape[0] // chunks
+    parts = [pl.ds(i * rows, rows) for i in range(chunks)]
+    copies = [
+        pltpu.make_async_copy(slots.at[part], slots_out.at[part], sem.at[i])
+        for i, part in enumerate(parts)
+    ]
+    copies.append(pltpu.make_async_copy(logits, logits_out, sem.at[chunks]))
+    copies.append(pltpu.make_async_copy(router, router_out, sem.at[chunks + 1]))
+    for copy in copies:
+        copy.start()
+    for copy in copies:
+        copy.wait()
 
 
 def on_device(expert_rows, expert_ids, gate_logits, layer_input, out_grad):
@@ -368,9 +395,9 @@
     slot_grad, logit_grad, router_grad = pl.pallas_call(
         functools.partial(kernel, n_dp, n_tensor, (tokens * n_dp * n_tensor) ** -0.5),
         out_shape=(
-            jax.ShapeDtypeStruct((slot_count, span), BF16),
-            jax.ShapeDtypeStruct((2, tokens), F32),
-            jax.ShapeDtypeStruct((owned, EXPERTS), F32),
+            pltpu.VMEM((slot_count, span), BF16),
+            pltpu.VMEM((2, tokens), F32),
+            pltpu.VMEM((owned, EXPERTS), F32),
         ),
         in_specs=[any_space, in_vmem, in_vmem, any_space, any_space],
         out_specs=(in_vmem, in_vmem, in_vmem),
@@ -392,12 +419,12 @@
             dma((3,)),
             dma((n_tensor,)),
             dma((n_tensor,)),
-            dma((n_tensor,)),
-            dma((n_tensor,)),
-            dma((n_dp,)),
-            dma((n_dp,)),
-            dma((n_tensor,)),
-            dma((n_tensor,)),
+            dma,
+            dma,
+            dma,
+            dma,
+            dma,
+            dma,
         ],
         compiler_params=pltpu.CompilerParams(
             collective_id=0, has_side_effects=True, vmem_limit_bytes=56 * 2**20
@@ -409,6 +436,19 @@
         layer_input,
         out_grad,
     )
+    chunks = 6
+    slot_grad, logit_grad, router_grad = pl.pallas_call(
+        functools.partial(hand_over, chunks),
+        out_shape=(
+            jax.ShapeDtypeStruct((slot_count, span), BF16),
+            jax.ShapeDtypeStruct((2, tokens), F32),
+            jax.ShapeDtypeStruct((owned, EXPERTS), F32),
+        ),
+        in_specs=[any_space] * 3,
+        out_specs=(any_space,) * 3,
+        scratch_shapes=[dma((chunks + 2,))],
+        compiler_params=pltpu.CompilerParams(vmem_limit_bytes=2**20),
+    )(slot_grad, logit_grad, router_grad)
     return slot_grad.reshape(expert_rows.shape), logit_grad.T, router_grad
 
 

time: 87.8 us -> 81.8 us (0.932)
  local copies, waits for them, and re-layouts: 3.84 us -> 0 us
  Pallas kernels: 83.1 us -> 81 us
    unnamed x7 -> x0, local copies, waits for them, and re-layouts: 3.84 us -> none
    pallas_call x1, Pallas kernels: 83.1 us -> 79.7 us  [on_device(): pl.pallas_call(functools.partial(kernel, n_dp, n_tensor, (tokens * n_dp *...]
    pallas_call x0 -> x1, Pallas kernels: none -> 1.23 us  [on_device(): pl.pallas_call(functools.partial(hand_over, chunks), out_shape=(jax.Shape...]
where the time goes in v2:
time: 81.8 us; the launch traced here: 81.6 us
  Pallas kernels  81 us (99%)
    pallas_call x1, Pallas kernels, on_device(): pl.pallas_call(functools.partial(kernel, n_dp, n_tensor, (tokens * n_dp *...  79.7 us

profile of v2, /device:TPU:1, one launch (start us, length us, event | category | flops | bytes accessed | tf_op | source)
XLA Modules:
  0.0 81.6 jit_solution(2450885579196981224)
XLA Ops:
  0.6 79.7 %shard_map.76 = (bf16[1056,768]{1,0:T(8,128)(2,1)S(1)}, f32[2,128]{1,0:T(2,128)S(1)}, f32[4,8]{1,0:T(4,128)S(1)}) custom-call(bf16[1056,768]{1,0:T(8,128)(2,1)} %bitcast.5, s32[2,128]{1,0:T(2,128)} %bitcast.6, f32[2,128]{1,0:T(2,128)} %bitcast.7, bf16[128,3072]{1,0:T(8,128)(2,1)} %input_hbm.1, bf16[128,3072]{1,0:T(8,128)(2,1)} %grad_hbm.1), custom_call_target="tpu_custom_call" | custom-call | tf_op jit(solution)/shard_map/pallas_call | solution.py:395
  80.4 1.2 %shard_map.77 = (bf16[1056,768]{1,0:T(8,128)(2,1)}, f32[2,128]{1,0:T(2,128)}, f32[4,8]{1,0:T(4,128)}) custom-call(bf16[1056,768]{1,0:T(8,128)(2,1)S(1)} %get-tuple-element.9.slots, f32[2,128]{1,0:T(2,128)S(1)} %get-tuple-element.10.logits, f32[4,8]{1,0:T(4,128)S(1)} %get-tuple-element.11.router), custom_call_target="tpu_custom_call" | custom-call | tf_op jit(solution)/shard_map/pallas_call | solution.py:440

commit v3 on v2

--- a/solution.py
+++ b/solution.py
@@ -33,13 +33,15 @@
     n_tensor,
     scale,
     rows_hbm,
-    ids_ref,
-    logits_ref,
+    ids_hbm,
+    logits_hbm,
     input_hbm,
     grad_hbm,
     slot_out,
     logit_out,
     router_out,
+    ids_ref,
+    logits_ref,
     rows,
     inputs,
     grads,
@@ -47,6 +49,8 @@
     recv,
     rows32,
     slot32,
+    mine_last,
+    other_last,
     score_send,
     score_recv,
     term_send,
@@ -63,6 +67,10 @@
     trecv_sem,
     psend_sem,
     precv_sem,
+    lsend_sem,
+    lrecv_sem,
+    fsend_sem,
+    frecv_sem,
 ):
     me = lax.axis_index("tensor")
     group = lax.axis_index("dp")
@@ -81,22 +89,29 @@
     def dp_peer(i):
         return wrapped(group + i, n_dp)
 
-    @pl.loop(1, n_tensor, unroll=True)
-    def _(i):
-        pl.semaphore_signal(
-            barrier, inc=1, device_id={"tensor": tensor_peer(i)}, device_id_type=MESH
-        )
-
-    @pl.loop(1, n_dp, unroll=True)
-    def _(i):
-        pl.semaphore_signal(barrier, inc=1, device_id={"dp": dp_peer(i)}, device_id_type=MESH)
-
+    load_ids = pltpu.make_async_copy(ids_hbm, ids_ref, load_sem.at[3])
+    load_logits = pltpu.make_async_copy(logits_hbm, logits_ref, load_sem.at[4])
     load_grads = pltpu.make_async_copy(grad_hbm, grads, load_sem.at[0])
     load_rows = pltpu.make_async_copy(rows_hbm, rows, load_sem.at[1])
     load_inputs = pltpu.make_async_copy(input_hbm, inputs, load_sem.at[2])
+    load_ids.start()
+    load_logits.start()
     load_grads.start()
+
+    @pl.loop(1, n_tensor, unroll=True)
+    def _(i):
+        pl.semaphore_signal(
+            barrier, inc=1, device_id={"tensor": tensor_peer(i)}, device_id_type=MESH
+        )
+
+    @pl.loop(1, n_dp, unroll=True)
+    def _(i):
+        pl.semaphore_signal(barrier, inc=1, device_id={"dp": dp_peer(i)}, device_id_type=MESH)
+
     load_rows.start()
     load_inputs.start()
+    load_ids.wait()
+    load_logits.wait()
 
     id0, id1 = ids_ref[0:1, :], ids_ref[1:2, :]
     logit0, logit1 = logits_ref[0:1, :], logits_ref[1:2, :]
@@ -113,21 +128,50 @@
     rank1 = jnp.sum(hot1 * before, axis=0, keepdims=True).astype(jnp.int32)
     slots = iota((LANES, tokens), 0)
     tail_row = iota((16, LANES), 0)
+    prob_row = 2 * segments
 
     load_grads.wait()
     pl.semaphore_wait(barrier, n_tensor - 1 + n_dp - 1)
 
-    def remote_block(index, peer):
+    column, row, core = me // 8, lax.rem(me // 2, 4), lax.rem(me, 2)
+    sibling = me + 1 - 2 * core
+    tails = pl.ds(0, n_tensor // 2)
+    main = pl.ds(0, body)
+    last_tile = pl.ds(body, 16)
+
+    def remote(source, target, sent, received, peer):
         return pltpu.make_async_remote_copy(
-            src_ref=send.at[peer],
-            dst_ref=recv.at[index],
-            send_sem=send_sem.at[peer],
-            recv_sem=recv_sem.at[index],
+            src_ref=source,
+            dst_ref=target,
+            send_sem=sent,
+            recv_sem=received,
             device_id={"tensor": peer},
             device_id_type=MESH,
         )
 
-    column, row, core = me // 8, lax.rem(me // 2, 4), lax.rem(me, 2)
+    def for_block(peer, act):
+        @pl.when(lax.rem(peer, 2) == core)
+        def _():
+            act(remote(send.at[peer], recv.at[me], send_sem.at[peer], recv_sem.at[me], peer))
+
+        @pl.when(lax.rem(peer, 2) != core)
+        def _():
+            act(
+                remote(
+                    send.at[peer, main],
+                    recv.at[me, main],
+                    send_sem.at[peer],
+                    recv_sem.at[me],
+                    peer,
+                )
+            )
+
+    def start_block(peer):
+        for_block(peer, lambda copy: copy.start())
+
+    def sent_block(peer):
+        for_block(peer, lambda copy: copy.wait_send())
+
 
     def partner(i, sign):
         part, place = i // 8, i - 8
@@ -148,9 +192,9 @@
         prob = jnp.where(id0 == expert, prob0, jnp.where(id1 == expert, prob1, 0.0))
         hi, mid, lo = split3(prob)
         parts = jnp.where(
-            tail_row == segments,
+            tail_row == prob_row,
             hi,
-            jnp.where(tail_row == segments + 1, mid, jnp.where(tail_row == segments + 2, lo, 0.0)),
+            jnp.where(tail_row == prob_row + 1, mid, jnp.where(tail_row == prob_row + 2, lo, 0.0)),
         ).astype(BF16)
         slot_probs = lax.dot_general(
             parts, placing, (((1,), (1,)), ((), ())), preferred_element_type=F32
@@ -162,30 +206,37 @@
                 grads[:, k * segments * LANES : (k + 1) * segments * LANES],
                 preferred_element_type=F32,
             )
-            tail = slot_probs
+            if k % 2 == 0:
+                tail = slot_probs
             for j in range(segments):
                 piece = packed[:, j * LANES : (j + 1) * LANES]
                 send[peer, j * full : (j + 1) * full, :] = piece[:full].astype(BF16)
-                tail = jnp.where(tail_row == j, piece[full : full + 1], tail)
-            send[peer, body : body + 16, :] = tail.astype(BF16)
+                place = k % 2 * segments + j
+                tail = jnp.where(tail_row == place, piece[full : full + 1], tail)
+            if k % 2 == 1:
+                send[peer - 1 + core, body : body + 16, :] = tail.astype(BF16)
 
     half = row // 2
 
     @pl.loop(0, 4)
     def _(i):
         pack(lax.rem(column + i + 1, 4) * 2 + 1 - half)
-        remote_block(me, partner(2 * i, 1)).start()
-        remote_block(me, partner(2 * i + 1, 1)).start()
+        start_block(partner(2 * i, 1))
+        start_block(partner(2 * i + 1, 1))
 
     @pl.loop(0, 4)
     def _(i):
         pack(lax.rem(column + i + 1, 4) * 2 + half)
 
-    @pl.loop(8, n_tensor - 1)
-    def _(i):
-        remote_block(me, partner(i, 1)).start()
+    @pl.loop(24, n_tensor - 1)
+    def _(i):
+        start_block(partner(i, 1))
 
     pltpu.make_async_copy(send.at[me], recv.at[me], recv_sem.at[me]).start()
+
+    @pl.loop(8, 24)
+    def _(i):
+        start_block(partner(i, 1))
 
     load_rows.wait()
 
@@ -196,6 +247,18 @@
             rows32[j, pl.ds(at, 32), :] = rows[
                 pl.ds(at, 32), j * LANES : (j + 1) * LANES
             ].astype(F32)
+
+    line_row = iota((8, LANES), 0)
+
+    @pl.loop(0, n_tensor)
+    def _(i):
+        tile = jnp.zeros((8, LANES), F32)
+        for j in range(segments):
+            tile = jnp.where(line_row == j, rows32[j, pl.ds(i * capacity + full, 1), :], tile)
+        mine_last[i] = tile
+
+    exchange = remote(mine_last, other_last, lsend_sem, lrecv_sem, sibling)
+    exchange.start()
 
     diagonal = iota((full, LANES), 0) == iota((full, LANES), 1)
     lane = iota((1, LANES), 1)
@@ -210,32 +273,48 @@
             device_id_type=MESH,
         )
 
+    exchange.wait_recv()
+
     @pl.loop(0, n_tensor)
     def _(i):
-        source = partner(i, -1)
-        pltpu.make_async_copy(send.at[source], recv.at[source], recv_sem.at[source]).wait()
+        source = partner(lax.rem(i + 24, n_tensor), -1)
+        same = lax.rem(source, 2) == core
+
+        @pl.when(same)
+        def _():
+            pltpu.make_async_copy(send.at[source], recv.at[source], recv_sem.at[source]).wait()
+
+        @pl.when(lax.rem(source, 2) != core)
+        def _():
+            pltpu.make_async_copy(
+                send.at[source, main], recv.at[source, main], recv_sem.at[source]
+            ).wait()
+
         at = source * capacity
-        tail = recv[source, body : body + 16, :].astype(F32)
-        prob = (
-            tail[segments : segments + 1]
-            + tail[segments + 1 : segments + 2]
-            + tail[segments + 2 : segments + 3]
-        )
-        prob_column = jnp.sum(jnp.where(diagonal, prob, 0.0), axis=1, keepdims=True)
-        prob_last = jnp.sum(jnp.where(lane == full, prob, 0.0), axis=1, keepdims=True)
         products = jnp.zeros((full, LANES), F32)
-        last = jnp.zeros((1, LANES), F32)
         for j in range(segments):
             piece = recv[source, j * full : (j + 1) * full, :].astype(F32)
             products += piece * rows32[j, pl.ds(at, full), :]
-            slot32[j, pl.ds(at, full), :] = piece * prob_column
-            row = tail[j : j + 1]
-            last += row * rows32[j, pl.ds(at + full, 1), :]
-            slot32[j, pl.ds(at + full, 1), :] = row * prob_last
         sums = jnp.sum(products, axis=1, keepdims=True)
         line = jnp.sum(jnp.where(diagonal, sums, 0.0), axis=0, keepdims=True)
-        last_sum = jnp.sum(last, axis=1, keepdims=True)
-        score_send[source] = jnp.where(lane == full, last_sum, line)
+        score_send[source] = line
+
+        @pl.when(same)
+        def _():
+            remote(
+                recv.at[source, last_tile],
+                recv.at[source, last_tile],
+                fsend_sem,
+                frecv_sem,
+                sibling,
+            ).start()
+            tail = recv[source, body : body + 16, :].astype(F32)
+            mine, other = mine_last[source], other_last[source]
+            first = jnp.where(core == 0, mine, other)
+            second = jnp.where(core == 0, other, mine)
+            last = tail[:8] * first + tail[segments : segments + 8] * second
+            last_sum = jnp.sum(jnp.sum(last, axis=0, keepdims=True), axis=1, keepdims=True)
+            score_send[source] = jnp.where(lane == full, last_sum, line)
 
         @pl.when(source != me)
         def _():
@@ -260,12 +339,11 @@
             total += score_recv[expert * members + k]
         scores = jnp.where(iota((EXPERTS, LANES), 0) == expert, total, scores)
     hi, mid, lo = split3(scores)
-    terms = [part.astype(BF16) for part in (hi, mid, lo)]
+    terms = jnp.concatenate([hi, mid, lo, jnp.zeros_like(lo)], axis=0).astype(BF16)
 
     def looked_up(chosen, hot):
-        found = jnp.zeros((EXPERTS, tokens), F32)
-        for term in terms:
-            found += jnp.dot(term, chosen, preferred_element_type=F32)
+        found = jnp.dot(terms, chosen, preferred_element_type=F32)
+        found = found[:EXPERTS] + found[EXPERTS : 2 * EXPERTS] + found[2 * EXPERTS : 3 * EXPERTS]
         return jnp.sum(found * hot, axis=0, keepdims=True)
 
     score0 = looked_up(chosen0, hot0)
@@ -305,6 +383,25 @@
     )
     own_term.start()
 
+    pltpu.make_async_copy(send.at[tails, last_tile], recv.at[tails, last_tile], frecv_sem).wait()
+
+    @pl.loop(0, n_tensor)
+    def _(i):
+        at = i * capacity
+        tail = recv[i, body : body + 16, :].astype(F32)
+        prob = (
+            tail[prob_row : prob_row + 1]
+            + tail[prob_row + 1 : prob_row + 2]
+            + tail[prob_row + 2 : prob_row + 3]
+        )
+        prob_column = jnp.sum(jnp.where(diagonal, prob, 0.0), axis=1, keepdims=True)
+        prob_last = jnp.sum(jnp.where(lane == full, prob, 0.0), axis=1, keepdims=True)
+        lasts = jnp.where(core == 0, tail[:8], tail[segments : segments + 8]) * prob_last
+        for j in range(segments):
+            piece = recv[i, j * full : (j + 1) * full, :].astype(F32)
+            slot32[j, pl.ds(at, full), :] = piece * prob_column
+            slot32[j, pl.ds(at + full, 1), :] = lasts[j : j + 1]
+
     @pl.loop(0, rows.shape[0] // 32)
     def _(i):
         at = pl.multiple_of(i * 32, 32)
@@ -346,7 +443,12 @@
 
     @pl.loop(1, n_tensor)
     def _(i):
-        remote_block(me, tensor_peer(i)).wait_send()
+        sent_block(tensor_peer(i))
+
+    remote(mine_last, other_last, lsend_sem, lrecv_sem, sibling).wait_send()
+    pltpu.make_async_copy(
+        send.at[tails, last_tile], recv.at[tails, last_tile], fsend_sem
+    ).wait()
 
     others = pl.ds(0, n_tensor - 1)
     pltpu.make_async_copy(score_send.at[others], score_recv.at[others], ssend_sem).wait()
@@ -399,9 +501,11 @@
             pltpu.VMEM((2, tokens), F32),
             pltpu.VMEM((owned, EXPERTS), F32),
         ),
-        in_specs=[any_space, in_vmem, in_vmem, any_space, any_space],
+        in_specs=[any_space] * 5,
         out_specs=(in_vmem, in_vmem, in_vmem),
         scratch_shapes=[
+            pltpu.VMEM((2, tokens), jnp.int32),
+            pltpu.VMEM((2, tokens), F32),
             pltpu.VMEM((slot_count, span), BF16),
             pltpu.VMEM((tokens, width), BF16),
             pltpu.VMEM((tokens, width), BF16),
@@ -409,6 +513,8 @@
             pltpu.VMEM((n_tensor, block, LANES), BF16),
             pltpu.VMEM((segments, padded, LANES), F32),
             pltpu.VMEM((segments, padded, LANES), F32),
+            pltpu.VMEM((n_tensor, 8, LANES), F32),
+            pltpu.VMEM((n_tensor, 8, LANES), F32),
             pltpu.VMEM((n_tensor, 1, LANES), F32),
             pltpu.VMEM((n_tensor, 1, LANES), F32),
             pltpu.VMEM((n_dp, EXPERTS, LANES), F32),
@@ -416,9 +522,13 @@
             pltpu.VMEM((LANES, LANES), F32),
             pltpu.VMEM((n_tensor, 1, LANES), F32),
             pltpu.VMEM((n_tensor, 1, LANES), F32),
-            dma((3,)),
+            dma((5,)),
             dma((n_tensor,)),
             dma((n_tensor,)),
+            dma,
+            dma,
+            dma,
+            dma,
             dma,
             dma,
             dma,

time: 81.8 us -> 79.9 us (0.977)
  Pallas kernels: 81 us -> 79.1 us
    pallas_call x1, Pallas kernels: 79.7 us -> 77.9 us  [on_device(): pl.pallas_call(functools.partial(kernel, n_dp, n_tensor, (tokens * n_dp *...]
where the time goes in v3:
time: 79.9 us; the launch traced here: 79.8 us
  Pallas kernels  79.1 us (99%)
    pallas_call x1, Pallas kernels, on_device(): pl.pallas_call(functools.partial(kernel, n_dp, n_tensor, (tokens * n_dp *...  77.9 us

profile of v3, /device:TPU:1, one launch (start us, length us, event | category | flops | bytes accessed | tf_op | source)
XLA Modules:
  0.0 79.8 jit_solution(14778065284933441248)
XLA Ops:
  0.6 77.9 %shard_map.76 = (bf16[1056,768]{1,0:T(8,128)(2,1)S(1)}, f32[2,128]{1,0:T(2,128)S(1)}, f32[4,8]{1,0:T(4,128)S(1)}) custom-call(bf16[1056,768]{1,0:T(8,128)(2,1)} %bitcast.5, s32[2,128]{1,0:T(2,128)} %bitcast.6, f32[2,128]{1,0:T(2,128)} %bitcast.7, bf16[128,3072]{1,0:T(8,128)(2,1)} %input_hbm.1, bf16[128,3072]{1,0:T(8,128)(2,1)} %grad_hbm.1), custom_call_target="tpu_custom_call" | custom-call | tf_op jit(solution)/shard_map/pallas_call | solution.py:497
  78.6 1.2 %shard_map.77 = (bf16[1056,768]{1,0:T(8,128)(2,1)}, f32[2,128]{1,0:T(2,128)}, f32[4,8]{1,0:T(4,128)}) custom-call(bf16[1056,768]{1,0:T(8,128)(2,1)S(1)} %get-tuple-element.9.slots, f32[2,128]{1,0:T(2,128)S(1)} %get-tuple-element.10.logits, f32[4,8]{1,0:T(4,128)S(1)} %get-tuple-element.11.router), custom_call_target="tpu_custom_call" | custom-call | tf_op jit(solution)/shard_map/pallas_call | solution.py:550

commit v4 on v3

--- a/solution.py
+++ b/solution.py
@@ -22,6 +22,13 @@
     hi = x.astype(BF16).astype(F32)
     mid = (x - hi).astype(BF16).astype(F32)
     return hi, mid, x - hi - mid
+
+
+def summed(parts):
+    while len(parts) > 1:
+        pairs = [a + b for a, b in zip(parts[::2], parts[1::2])]
+        parts = pairs + parts[len(pairs) * 2 :]
+    return parts[0]
 
 
 def wrapped(index, size):
@@ -89,6 +96,20 @@
     def dp_peer(i):
         return wrapped(group + i, n_dp)
 
+    column, row, core = me // 8, lax.rem(me // 2, 4), lax.rem(me, 2)
+
+    def partner(i, sign):
+        part, place = i // 8, i - 8
+        middle = (part == 1) | (part == 2)
+        along_y = jnp.where(middle, 1 + 2 * lax.rem(i, 2), jnp.where(part == 0, 2, 0))
+        rest = jnp.where(middle, place // 2, lax.rem(i, 8))
+        along_x = lax.rem(rest // 2 + 1, 4)
+        return (
+            lax.rem(column + sign * along_x + 4, 4) * 8
+            + lax.rem(row + sign * along_y + 4, 4) * 2
+            + lax.rem(core + rest + 1, 2)
+        )
+
     load_ids = pltpu.make_async_copy(ids_hbm, ids_ref, load_sem.at[3])
     load_logits = pltpu.make_async_copy(logits_hbm, logits_ref, load_sem.at[4])
     load_grads = pltpu.make_async_copy(grad_hbm, grads, load_sem.at[0])
@@ -98,10 +119,9 @@
     load_logits.start()
     load_grads.start()
 
-    @pl.loop(1, n_tensor, unroll=True)
-    def _(i):
+    for i in range(n_tensor - 1):
         pl.semaphore_signal(
-            barrier, inc=1, device_id={"tensor": tensor_peer(i)}, device_id_type=MESH
+            barrier, inc=1, device_id={"tensor": partner(i, 1)}, device_id_type=MESH
         )
 
     @pl.loop(1, n_dp, unroll=True)
@@ -133,7 +153,6 @@
     load_grads.wait()
     pl.semaphore_wait(barrier, n_tensor - 1 + n_dp - 1)
 
-    column, row, core = me // 8, lax.rem(me // 2, 4), lax.rem(me, 2)
     sibling = me + 1 - 2 * core
     tails = pl.ds(0, n_tensor // 2)
     main = pl.ds(0, body)
@@ -172,18 +191,6 @@
     def sent_block(peer):
         for_block(peer, lambda copy: copy.wait_send())
 
-
-    def partner(i, sign):
-        part, place = i // 8, i - 8
-        middle = (part == 1) | (part == 2)
-        along_y = jnp.where(middle, 1 + 2 * lax.rem(i, 2), jnp.where(part == 0, 2, 0))
-        rest = jnp.where(middle, place // 2, lax.rem(i, 8))
-        along_x = lax.rem(rest // 2 + 1, 4)
-        return (
-            lax.rem(column + sign * along_x + 4, 4) * 8
-            + lax.rem(row + sign * along_y + 4, 4) * 2
-            + lax.rem(core + rest + 1, 2)
-        )
 
     def pack(expert):
         key0 = jnp.where(id0 == expert, rank0, -1)
@@ -365,6 +372,16 @@
             device_id_type=MESH,
         )
 
+    def remote_term(index, peer):
+        return pltpu.make_async_remote_copy(
+            src_ref=term_send.at[peer],
+            dst_ref=term_recv.at[index],
+            send_sem=tsend_sem,
+            recv_sem=trecv_sem,
+            device_id={"dp": peer},
+            device_id_type=MESH,
+        )
+
     for k in range(members):
         term = jnp.dot(
             combined,
@@ -374,9 +391,20 @@
         for j in range(segments):
             term_send[k * segments + j] = term[:, j * LANES : (j + 1) * LANES]
 
-    @pl.loop(1, n_dp, unroll=True)
-    def _(i):
-        remote_term(group, dp_peer(i)).start()
+    for k in range(members):
+        term = jnp.dot(
+            combined,
+            inputs[:, k * segments * LANES : (k + 1) * segments * LANES],
+            preferred_element_type=F32,
+        )
+        for j in range(segments):
+            term_send[k * segments + j] = term[:, j * LANES : (j + 1) * LANES]
+        for j in range(segments):
+            peer = k * segments + j
+
+            @pl.when(group != peer)
+            def _(peer=peer):
+                remote_term(group, peer).start()
 
     own_term = pltpu.make_async_copy(
         term_send.at[group], term_recv.at[group], trecv_sem
@@ -411,9 +439,7 @@
             ].astype(BF16)
 
     pltpu.make_async_copy(term_send, term_recv, trecv_sem).wait()
-    total = term_recv[0]
-    for g in range(1, n_dp):
-        total += term_recv[g]
+    total = summed([term_recv[g] for g in range(n_dp)])
 
     square = jnp.concatenate([total, jnp.zeros((LANES - EXPERTS, LANES), F32)], axis=0)
     turned[...] = jnp.transpose(square)
@@ -456,10 +482,7 @@
     pltpu.make_async_copy(term_send.at[others_dp], term_recv.at[others_dp], tsend_sem).wait()
 
     pltpu.make_async_copy(part_send, part_recv, precv_sem).wait()
-    line = part_recv[0]
-    for i in range(1, n_tensor):
-        line += part_recv[i]
-    line = line * scale
+    line = summed([part_recv[i] for i in range(n_tensor)]) * scale
     for j in range(owned):
         router_out[j : j + 1, :] = line[:, j * EXPERTS : (j + 1) * EXPERTS]
 

time: 79.9 us -> 78.9 us (0.987)
  Pallas kernels: 79.1 us -> 78.1 us
    pallas_call x1, Pallas kernels: 77.9 us -> 76.9 us  [on_device(): pl.pallas_call(functools.partial(kernel, n_dp, n_tensor, (tokens * n_dp *...]
where the time goes in v4:
time: 78.9 us; the launch traced here: 78.7 us
  Pallas kernels  78.1 us (99%)
    pallas_call x1, Pallas kernels, on_device(): pl.pallas_call(functools.partial(kernel, n_dp, n_tensor, (tokens * n_dp *...  76.9 us

profile of v4, /device:TPU:1, one launch (start us, length us, event | category | flops | bytes accessed | tf_op | source)
XLA Modules:
  0.0 78.7 jit_solution(6934672300484080912)
XLA Ops:
  0.6 76.9 %shard_map.76 = (bf16[1056,768]{1,0:T(8,128)(2,1)S(1)}, f32[2,128]{1,0:T(2,128)S(1)}, f32[4,8]{1,0:T(4,128)S(1)}) custom-call(bf16[1056,768]{1,0:T(8,128)(2,1)} %bitcast.5, s32[2,128]{1,0:T(2,128)} %bitcast.6, f32[2,128]{1,0:T(2,128)} %bitcast.7, bf16[128,3072]{1,0:T(8,128)(2,1)} %input_hbm.1, bf16[128,3072]{1,0:T(8,128)(2,1)} %grad_hbm.1), custom_call_target="tpu_custom_call" | custom-call | tf_op jit(solution)/shard_map/pallas_call | solution.py:520
  77.5 1.2 %shard_map.77 = (bf16[1056,768]{1,0:T(8,128)(2,1)}, f32[2,128]{1,0:T(2,128)}, f32[4,8]{1,0:T(4,128)}) custom-call(bf16[1056,768]{1,0:T(8,128)(2,1)S(1)} %get-tuple-element.9.slots, f32[2,128]{1,0:T(2,128)S(1)} %get-tuple-element.10.logits, f32[4,8]{1,0:T(4,128)S(1)} %get-tuple-element.11.router), custom_call_target="tpu_custom_call" | custom-call | tf_op jit(solution)/shard_map/pallas_call | solution.py:573

commit v5 on v4

--- a/solution.py
+++ b/solution.py
@@ -124,8 +124,8 @@
             barrier, inc=1, device_id={"tensor": partner(i, 1)}, device_id_type=MESH
         )
 
-    @pl.loop(1, n_dp, unroll=True)
-    def _(i):
+    ring = n_dp // 2
+    for i in sorted(range(1, n_dp), key=lambda i: -min(i % ring, ring - i % ring)):
         pl.semaphore_signal(barrier, inc=1, device_id={"dp": dp_peer(i)}, device_id_type=MESH)
 
     load_rows.start()
@@ -382,25 +382,24 @@
             device_id_type=MESH,
         )
 
-    for k in range(members):
+    span = segments * LANES
+    quarter = group // segments
+    beside = quarter + 1 - 2 * lax.rem(quarter, 2)
+    for part in (
+        3 - quarter,
+        beside,
+        lax.rem(quarter + 2, 4),
+        quarter,
+    ):
         term = jnp.dot(
             combined,
-            inputs[:, k * segments * LANES : (k + 1) * segments * LANES],
+            inputs[:, pl.ds(pl.multiple_of(part * span, span), span)],
             preferred_element_type=F32,
         )
         for j in range(segments):
-            term_send[k * segments + j] = term[:, j * LANES : (j + 1) * LANES]
-
-    for k in range(members):
-        term = jnp.dot(
-            combined,
-            inputs[:, k * segments * LANES : (k + 1) * segments * LANES],
-            preferred_element_type=F32,
-        )
+            term_send[part * segments + j] = term[:, j * LANES : (j + 1) * LANES]
         for j in range(segments):
-            term_send[k * segments + j] = term[:, j * LANES : (j + 1) * LANES]
-        for j in range(segments):
-            peer = k * segments + j
+            peer = part * segments + j
 
             @pl.when(group != peer)
             def _(peer=peer):

time: 78.9 us -> 79.1 us (level)
  no operation moved by 1% of the time
where the time goes in v5:
time: 79.1 us; the launch traced here: 79 us
  Pallas kernels  78.3 us (99%)
    pallas_call x1, Pallas kernels, on_device(): pl.pallas_call(functools.partial(kernel, n_dp, n_tensor, (tokens * n_dp *...  77.1 us

profile of v5, /device:TPU:1, one launch (start us, length us, event | category | flops | bytes accessed | tf_op | source)
XLA Modules:
  0.0 79.0 jit_solution(1126676802829391371)
XLA Ops:
  0.6 77.1 %shard_map.76 = (bf16[1056,768]{1,0:T(8,128)(2,1)S(1)}, f32[2,128]{1,0:T(2,128)S(1)}, f32[4,8]{1,0:T(4,128)S(1)}) custom-call(bf16[1056,768]{1,0:T(8,128)(2,1)} %bitcast.5, s32[2,128]{1,0:T(2,128)} %bitcast.6, f32[2,128]{1,0:T(2,128)} %bitcast.7, bf16[128,3072]{1,0:T(8,128)(2,1)} %input_hbm.1, bf16[128,3072]{1,0:T(8,128)(2,1)} %grad_hbm.1), custom_call_target="tpu_custom_call" | custom-call | tf_op jit(solution)/shard_map/pallas_call | solution.py:519
  77.7 1.2 %shard_map.77 = (bf16[1056,768]{1,0:T(8,128)(2,1)}, f32[2,128]{1,0:T(2,128)}, f32[4,8]{1,0:T(4,128)}) custom-call(bf16[1056,768]{1,0:T(8,128)(2,1)S(1)} %get-tuple-element.9.slots, f32[2,128]{1,0:T(2,128)S(1)} %get-tuple-element.10.logits, f32[4,8]{1,0:T(4,128)S(1)} %get-tuple-element.11.router), custom_call_target="tpu_custom_call" | custom-call | tf_op jit(solution)/shard_map/pallas_call | solution.py:572
